TPU v7x, 32 devices: a whole 2x2x4 slice. The times are simulated.
32 devices in a mesh: groups: 2 (over x), sets: 8 (over z, y), mp: 2 (over core).
Axes of the slice: x: 2, y: 2, z: 4, core: 2. Of those that a mesh axis runs over, the one named last changes fastest.
Arguments:
- control: bfloat16 [8, 256, 2048], P('groups', 'sets'), parts along dimension 0, may hold values from -6 to 6
- line_ids: int32 [16], P(('groups', 'sets')), parts along dimension 0, may hold values from 0 to 3
- pert_ids: int32 [16], P('groups'), parts along dimension 0, may hold values from 0 to 2047
- pert_table: bfloat16 [2048, 2048], P('sets'), may hold values from -16 to 16
- blocks: int32 [16, 256], P(('groups', 'sets')), parts along dimension 0, may hold values from 0 to 3, never falling along the last dimension, each value on 1 to 128 neighbouring positions
- norm_gain: float32 [2048], replicated, may hold values from 0.1 to 1.9
- out_gain: float32 [2048], replicated, may hold values from 0.1 to 1.9
- qkv_weight: bfloat16 [2048, 3, 1024], P(None, None, 'mp'), may hold values from -1 to 1
- out_weight: bfloat16 [1024, 2048], P('mp'), may hold values from -0.75 to 0.75
- decoder: bfloat16 [2048, 12288], P('mp', 'sets'), may hold values from -0.125 to 0.125
Outputs:
- expression: bfloat16 [16, 256, 12288], P('groups', 'mp', 'sets'), parts along dimension 0
There are 2 independent parts, one for each index of `groups`. A program takes and returns all parts, laid end to end along the dimension named above; an argument that names none is the same for every part. Nothing has to cross between parts.
Inputs may be any that keep to these rules, and one draw needn't show every extreme that they name: `blocks`: in each set the ids never fall and form 4 runs of at most 128 cells.
All inputs are finite; a program needn't handle non-finite values.
Results may differ from a plain program's by a relative error of at most 0.0058.
Values may be sent and summed in bfloat16 or wider, within the bound.
A program may use at most 128 MiB of HBM per device.

v0:
```python
import jax
import jax.numpy as jnp
from jax import lax
from jax.sharding import PartitionSpec as P

HD = 128


def shards(
    control,
    line_ids,
    pert_ids,
    pert_table,
    blocks,
    norm_gain,
    out_gain,
    qkv_weight,
    out_weight,
    decoder,
):
    sets_here = line_ids.shape[0]
    line_count = control.shape[0]
    cell_count = blocks.shape[1]
    model_width = control.shape[2]
    line_range = jnp.arange(line_count, dtype=jnp.int32)
    picker = (line_ids[:, None] == line_range[None, :]).astype(jnp.bfloat16)
    chosen = jnp.einsum(
        "sl,lcd->scd",
        picker,
        lax.all_gather(control, "sets", axis=1, tiled=True),
        preferred_element_type=jnp.float32,
    )
    table_rows = pert_table.shape[0]
    offset = lax.axis_index("sets") * table_rows
    onehot = (
        pert_ids[:, None] == offset + jnp.arange(table_rows, dtype=jnp.int32)[None, :]
    ).astype(jnp.bfloat16)
    perturbed = lax.psum_scatter(
        jnp.dot(onehot, pert_table, preferred_element_type=jnp.float32).astype(jnp.bfloat16),
        "sets",
        scatter_dimension=0,
        tiled=True,
    ).astype(jnp.float32)
    stream = chosen + perturbed[:, None, :]
    mean_sq = jnp.mean(stream * stream, axis=2, keepdims=True)
    normed_in = (stream * lax.rsqrt(mean_sq + 1e-05) * norm_gain).astype(jnp.bfloat16)
    projected = jnp.einsum(
        "scd,dtk->sctk", normed_in, qkv_weight, preferred_element_type=jnp.float32
    ).astype(jnp.bfloat16)
    heads_here = projected.shape[3] // HD
    projected = projected.reshape(sets_here, cell_count, 3, heads_here, HD)
    queries = projected[:, :, 0]
    keys_here = projected[:, :, 1]
    values_here = projected[:, :, 2]
    scores = jnp.einsum(
        "sqhe,skhe->shqk", queries, keys_here, preferred_element_type=jnp.float32
    ) * HD ** (-0.5)
    same_block = (blocks[:, :, None] == blocks[:, None, :])[:, None]
    scores = jnp.where(same_block, scores, -1e30)
    weights = jax.nn.softmax(scores, axis=-1).astype(jnp.bfloat16)
    attended = jnp.einsum(
        "shqk,skhe->sqhe", weights, values_here, preferred_element_type=jnp.float32
    ).astype(jnp.bfloat16)
    attended = attended.reshape(sets_here, cell_count, heads_here * HD)
    partial_value = jnp.einsum(
        "sci,id->scd", attended, out_weight, preferred_element_type=jnp.float32
    )
    half_width = model_width // lax.axis_size("mp")
    own_start = lax.axis_index("mp") * half_width
    residual = lax.dynamic_slice_in_dim(stream, own_start, half_width, 2) + lax.psum_scatter(
        partial_value, "mp", scatter_dimension=2, tiled=True
    )
    squares = lax.psum(jnp.sum(residual * residual, axis=2, keepdims=True), "mp")
    gain_half = lax.dynamic_slice_in_dim(out_gain, own_start, half_width, 0)
    normed = (residual * lax.rsqrt(squares / model_width + 1e-05) * gain_half).astype(jnp.bfloat16)
    gene_terms = jnp.einsum(
        "scd,dg->scg",
        lax.all_gather(normed, "sets", axis=0, tiled=True),
        decoder,
        preferred_element_type=jnp.float32,
    )
    return lax.psum_scatter(gene_terms, "mp", scatter_dimension=1, tiled=True).astype(jnp.bfloat16)


def solution(mesh):
    placed = (
        P("groups", "sets", None),
        P(("groups", "sets")),
        P("groups"),
        P("sets", None),
        P(("groups", "sets"), None),
        P(),
        P(),
        P(None, None, "mp"),
        P("mp", None),
        P("mp", "sets"),
    )
    return jax.shard_map(
        shards, mesh=mesh, in_specs=placed, out_specs=P("groups", "mp", "sets"), check_vma=False
    )
```

profile of v0, /device:TPU:0, one launch (start us, length us, event | category | flops | bytes accessed | tf_op | source)
XLA Modules:
  0.0 247.4 jit_solution(10823132596918803817)
XLA Ops:
  6.5 0.7 all-gather.3.cloned.1.call-update
  7.3 0.0 reduce-scatter.3.cloned.1.call-start
  8.1 1.2 dynamic-slice.4
  9.4 1.5 convolution_convert_fusion
  10.9 39.7 %all-reduce = bf16[8,2048]{1,0:T(8,128)(2,1)S(1)} all-reduce(bf16[8,2048]{1,0:T(8,128)(2,1)S(1)} %convolution_convert_fusion), channel_id=2, replica_groups=mesh['groups'=2,'sets'=8,'mp'=2] {'sets'}, use_global_device_ids=true, to_apply=%region_0.0.clone | all-reduce | flops 16384 | bytes 65536
  50.6 0.7 dynamic-slice_convert_fusion
  51.2 0.9 broadcast_compare_fusion
  52.1 34.0 %all-gather.3.cloned.1.call-done = bf16[4,256,2048]{2,1,0:T(8,128)(2,1)} async-done(((bf16[4,32,2048]{2,1,0:T(8,128)(2,1)}), bf16[4,256,2048]{2,1,0:T(8,128)(2,1)}) %all-gather.3.cloned.1.call-update) | async-done | bytes 4194320 | tf_op jit(solution)/shard_map/all_gather | solution.py:30
  86.1 5.5 %fusion.1 = f32[1,256,2048]{2,0,1:T(1,128)S(1)} fusion(bf16[4,256,2048]{2,1,0:T(8,128)(2,1)} %all-gather.3.cloned.1.call-done, s32[]{:T(128)} %bitcast.56), kind=kOutput, calls=%fused_computation.1 | convolution fusion | flops 4194308 | bytes 6291460 | tf_op jit(solution)/shard_map/sl,lcd->scd/dot_general | solution.py:27
  91.6 0.9 multiply_reduce_fusion
  92.5 1.3 copy-done.1
  93.9 5.5 %convolution_convert_fusion.1 = bf16[256,3,512]{2,0,1:T(8,128)(2,1)} fusion(bf16[2048,3,512]{2,0,1:T(8,128)(2,1)} %param.17, f32[256,2048]{1,0:T(8,128)S(1)} %get-tuple-element.6, f32[2048]{0:T(1024)S(1)} %copy-done.2, f32[256]{0:T(256)S(1)} %add_rsqrt_fusion.1), kind=kOutput, calls=%fused_computation.11 | convolution fusion | flops 1612578816 | bytes 9184256 | tf_op jit(solution)/shard_map/scd,dtk->sctk/dot_general | solution.py:47
  99.4 2.4 reshape.138
  101.8 2.2 fusion.21
  104.0 1.4 fusion.22
  105.5 2.2 fusion.7
  107.7 1.8 copy.26
  109.6 2.0 convolution_convert_fusion.2
  111.6 3.6 %convolution_bitcast_fusion = f32[1,256,2048]{2,1,0:T(8,128)} fusion(bf16[256,512]{0,1:T(8,128)(2,1)S(1)} %bitcast.57, bf16[512,2048]{1,0:T(8,128)(2,1)} %param.18), kind=kOutput, calls=%fused_computation.5 | convolution fusion | flops 536870912 | bytes 4456448 | tf_op jit(solution)/shard_map/sci,id->scd/dot_general | solution.py:65
  115.2 0.0 reduce-scatter.3.cloned.1.call-update
  115.3 0.0 all-gather.5.cloned.1.call-start
  115.3 8.0 %reduce-scatter.3.cloned.1.call-done = f32[1,256,1024]{2,1,0:T(8,128)} async-done(((f32[1,256,2048]{2,1,0:T(8,128)}), f32[1,256,1024]{2,1,0:T(8,128)}) %reduce-scatter.3.cloned.1.call-update) | async-done | bytes 1048592 | tf_op jit(solution)/shard_map/reduce_scatter | solution.py:70
  123.3 1.7 multiply_reduce_fusion.1
  125.0 2.5 psum.7
  127.5 2.5 %multiply_convert_fusion.1 = bf16[1,256,1024]{2,1,0:T(8,128)(2,1)} fusion(f32[1024]{0:T(1024)S(1)} %dynamic-slice-done, f32[256]{0:T(256)S(1)} %bitcast.59, f32[1,256,1024]{2,1,0:T(8,128)} %reduce-scatter.3.cloned.1.call-done, f32[256,2048]{1,0:T(8,128)} %copy-done.1, s32[]{:T(128)} %select_n.9), kind=kLoop, calls=%fused_computation.18 | loop fusion | flops 1048576 | bytes 2626564 | tf_op jit(solution)/shard_map/convert_element_type | solution.py:75
  130.0 0.0 all-gather.5.cloned.1.call-update
  130.0 0.2 reduce-scatter.5.cloned.1.call-start
  130.3 74.5 %all-gather.5.cloned.1.call-done = bf16[8,256,1024]{2,1,0:T(8,128)(2,1)} async-done(((bf16[1,256,1024]{2,1,0:T(8,128)(2,1)}), bf16[8,256,1024]{2,1,0:T(8,128)(2,1)}) %all-gather.5.cloned.1.call-update) | async-done | bytes 4194320 | tf_op jit(solution)/shard_map/all_gather | solution.py:78
  204.8 11.3 %fusion.3 = f32[8,256,1536]{2,1,0:T(8,128)} fusion(bf16[8,256,1024]{2,1,0:T(8,128)(2,1)} %all-gather.5.cloned.1.call-done, bf16[1024,1536]{1,0:T(8,128)(2,1)S(1)} %copy-done), kind=kOutput, calls=%fused_computation.3 | convolution fusion | flops 6442450944 | bytes 19922944 | tf_op jit(solution)/shard_map/scd,dg->scg/dot_general | solution.py:76
  216.1 0.0 reduce-scatter.5.cloned.1.call-update
  216.1 19.9 %reduce-scatter.5.cloned.1.call-done = f32[8,128,1536]{2,1,0:T(8,128)} async-done(((f32[8,256,1536]{2,1,0:T(8,128)}), f32[8,128,1536]{2,1,0:T(8,128)}) %reduce-scatter.5.cloned.1.call-update) | async-done | bytes 6291472 | tf_op jit(solution)/shard_map/reduce_scatter | solution.py:82
  236.1 4.8 %convert_element_type.41 = bf16[8,128,1536]{2,1,0:T(8,128)(2,1)} convert(f32[8,128,1536]{2,1,0:T(8,128)} %reduce-scatter.5.cloned.1.call-done) | non-fusion elementwise | flops 1572864 | bytes 9437184 | tf_op jit(solution)/shard_map/convert_element_type | solution.py:82
  (11 shorter events, 0.0 us)
Async XLA Ops:
  6.5 198.2 %copy-start = (bf16[1024,1536]{1,0:T(8,128)(2,1)S(1)}, bf16[1024,1536]{1,0:T(8,128)(2,1)}, u32[]{:S(2)}) copy-start(bf16[1024,1536]{1,0:T(8,128)(2,1)} %param.19) | copy-start | bytes 9437188
  6.5 79.5 %all-gather.3.cloned.1.call-start = ((), (), s32[]{:S(2)}) async-start(), calls=%async_computation.2 | async-start | bytes 4718592 | tf_op jit(solution)/shard_map/all_gather | solution.py:30
  7.3 116.0 %reduce-scatter.3.cloned.1.call-start = ((), (), s32[]{:S(2)}) async-start(), calls=%async_computation.3 | async-start | bytes 3145728 | tf_op jit(solution)/shard_map/reduce_scatter | solution.py:70
  91.6 2.3 copy-start.2
  92.5 1.4 copy-start.1
  115.3 89.5 %all-gather.5.cloned.1.call-start = ((), (), s32[]{:S(2)}) async-start(), calls=%async_computation.4 | async-start | bytes 4718592 | tf_op jit(solution)/shard_map/all_gather | solution.py:78
  115.3 12.2 %dynamic-slice-start = ((f32[2048]{0:T(1024)}, s32[]{:T(128)}), f32[1024]{0:T(1024)S(1)}, s32[]{:S(2)}) async-start(f32[2048]{0:T(1024)} %param.16, s32[]{:T(128)} %select_n.9), calls=%async_computation.6 | async-start | bytes 8704 | tf_op jit(solution)/shard_map/dynamic_slice | solution.py:74
  130.0 106.0 %reduce-scatter.5.cloned.1.call-start = ((), (), s32[]{:S(2)}) async-start(), calls=%async_computation.5 | async-start | bytes 18874368 | tf_op jit(solution)/shard_map/reduce_scatter | solution.py:82
Sparse Core Ops, SparseCore 0:
  9.5 76.4 all-gather.2
  115.4 7.8 reduce-scatter.2
  130.2 74.5 all-gather.4
  216.2 19.7 reduce-scatter.4
where the time goes:
time: 248 us; the launch traced here: 247 us
  waiting for transfers between devices  137 us (55%)
  blocking collectives  42.1 us (17%)
  matrix products  33.2 us (13%)
  between operations  14 us (6%)
  other arithmetic  11.5 us (5%)
  local copies, waits for them, and re-layouts  9.06 us (4%)
    all_gather x1, waiting for transfers between devices, shards(): lax.all_gather(normed, 'sets', axis=0, tiled=True)  74.5 us
    unnamed x1, blocking collectives  39.7 us
    all_gather x1, waiting for transfers between devices, shards(): lax.all_gather(control, 'sets', axis=1, tiled=True)  34 us
    reduce_scatter x1, waiting for transfers between devices, shards(): lax.psum_scatter(gene_terms, 'mp', scatter_dimension=1, tiled=True)  19.9 us
    dot_general x1, matrix products, shards(): jnp.einsum('scd,dg->scg', lax.all_gather(normed, 'sets', axis=0, tiled=Tr...  11.3 us
    reduce_scatter x1, waiting for transfers between devices, shards(): lax.psum_scatter(partial_value, 'mp', scatter_dimension=2, tiled=True)  7.97 us
    dot_general x1, matrix products, shards(): jnp.einsum('scd,dtk->sctk', normed_in, qkv_weight, preferred_element_type...  5.53 us
    dot_general x1, matrix products, shards(): jnp.einsum('sl,lcd->scd', picker, lax.all_gather(control, 'sets', axis=1,...  5.49 us
  transfers between devices with their start and end apart: 4, of which 4 were waited for; matrix products, arithmetic and copies ran while one was open for 2% of the time, Pallas kernels for 0%

commit v1 on v0

v1 whole, which is shorter than its diff:
```python
import functools

import jax
import jax.numpy as jnp
from jax import lax
from jax.experimental import pallas as pl
from jax.experimental.pallas import tpu as pltpu
from jax.sharding import PartitionSpec as P

HD = 128
MESH = pl.DeviceIdType.MESH
MIB = 1024 * 1024


def gather_kernel(n, payload, qkv, outw, dec, cells, qkv_all, outw_all, dec_all,
                  send, recv, wsend, wrecv, local):
    nz = n // 2
    me = lax.axis_index("sets")
    m = lax.axis_index("mp")
    z, y = me // 2, me % 2
    peer = {"mp": 1 - m}
    other = {"sets": z * 2 + 1 - y}
    up = {"sets": jnp.minimum(z + 1, nz - 1) * 2 + y}
    down = {"sets": jnp.maximum(z - 1, 0) * 2 + y}

    barrier = pltpu.get_barrier_semaphore()
    pl.semaphore_signal(barrier, inc=1, device_id=peer, device_id_type=MESH)
    pl.semaphore_signal(barrier, inc=1, device_id=other, device_id_type=MESH)

    @pl.when(z < nz - 1)
    def _():
        pl.semaphore_signal(barrier, inc=1, device_id=up, device_id_type=MESH)

    @pl.when(z > 0)
    def _():
        pl.semaphore_signal(barrier, inc=1, device_id=down, device_id_type=MESH)

    own = [
        pltpu.make_async_copy(payload, cells.at[m, me], local.at[0]),
        pltpu.make_async_copy(qkv, qkv_all.at[m], local.at[1]),
        pltpu.make_async_copy(outw, outw_all.at[m], local.at[2]),
        pltpu.make_async_copy(dec, dec_all.at[m], local.at[3]),
    ]
    for copy in own:
        copy.start()

    neighbours = 2 + jnp.where(z < nz - 1, 1, 0) + jnp.where(z > 0, 1, 0)
    pl.semaphore_wait(barrier, neighbours)

    def move(src, d, target, lane):
        return pltpu.make_async_remote_copy(
            src_ref=src,
            dst_ref=cells.at[m, d],
            send_sem=send.at[d, lane],
            recv_sem=recv.at[m, d],
            device_id=target,
            device_id_type=MESH,
        )

    def landed(half, d):
        pltpu.make_async_remote_copy(
            src_ref=cells.at[half, d],
            dst_ref=cells.at[half, d],
            send_sem=send.at[d, 0],
            recv_sem=recv.at[half, d],
            device_id=peer,
            device_id_type=MESH,
        ).wait_recv()

    def each(source, act):
        for k in range(nz):
            for sign in ((0,) if k == 0 else (-1, 1)):
                at = z + sign * k

                @pl.when((at >= 0) & (at < nz))
                def _(at=at, sign=sign, k=k):
                    d = at * 2 + y
                    src = source(d, k)
                    if sign <= 0:

                        @pl.when(z < nz - 1)
                        def _():
                            act(move(src, d, up, 0))

                    if sign >= 0:

                        @pl.when(z > 0)
                        def _():
                            act(move(src, d, down, 1))

                    act(move(src, d, other, 2))
                    act(move(src, d, peer, 3))

            if k == 0:
                after_own()
            crossing(k, act)

    def crossing(k, act):
        for sign in ((0,) if k == 0 else (-1, 1)):
            at = z + sign * k

            @pl.when((at >= 0) & (at < nz))
            def _(at=at):
                d = at * 2 + 1 - y
                if act is start:
                    landed(m, d)
                act(move(cells.at[m, d], d, peer, 3))

    weights = [
        pltpu.make_async_remote_copy(
            src_ref=src,
            dst_ref=dst.at[m],
            send_sem=wsend.at[i],
            recv_sem=wrecv.at[i],
            device_id=peer,
            device_id_type=MESH,
        )
        for i, (src, dst) in enumerate(((qkv, qkv_all), (outw, outw_all), (dec, dec_all)))
    ]

    def start(copy):
        copy.start()

    def finish(copy):
        copy.wait_send()

    def source(d, k):
        if k == 0:
            return payload
        landed(m, d)
        return cells.at[m, d]

    def after_own():
        for copy in weights:
            copy.start()

    each(source, start)

    def source(d, k):
        return payload if k == 0 else cells.at[m, d]

    def after_own():
        pass

    each(source, finish)

    for d in range(n):
        landed(1 - m, d)
    for copy in weights:
        copy.wait()
    for copy in own:
        copy.wait()


def project_kernel(rows_ref, weight_ref, out_ref):
    out_ref[...] = jnp.dot(
        rows_ref[...], weight_ref[0, 0], preferred_element_type=jnp.float32
    )


def layer_kernel(pair, width, idx_ref, *refs):
    ins, (gain_ref, outw_ref, dec_ref, out_ref, att, res) = refs[: 9 * pair], refs[9 * pair :]
    half = att.shape[0] // pair
    inner = att.shape[1]
    for j in range(pair):
        c_ref, own_ref, p_ref, q_ref, k_ref, v_ref, b_ref, row_ref, col_ref = ins[9 * j : 9 * j + 9]
        p = p_ref[0]
        stream = c_ref[0].astype(jnp.float32) + p
        scale = lax.rsqrt(jnp.sum(stream * stream, axis=1, keepdims=True) / width + 1e-05)
        own = own_ref[0].astype(jnp.float32) + p
        own_scale = lax.rsqrt(jnp.sum(own * own, axis=1, keepdims=True) / width + 1e-05)
        res[j * half : (j + 1) * half, :] = own
        same = col_ref[0] == row_ref[0]
        b = b_ref[0]
        for h in range(inner // HD):
            part = slice(h * HD, (h + 1) * HD)
            q = (own_scale * (q_ref[:, part] + b[:, part])).astype(jnp.bfloat16)
            k = (scale * (k_ref[:, part] + b[:, inner + h * HD : inner + (h + 1) * HD])).astype(jnp.bfloat16)
            v = (scale * (v_ref[:, part] + b[:, 2 * inner + h * HD : 2 * inner + (h + 1) * HD])).astype(jnp.bfloat16)
            s = lax.dot_general(q, k, (((1,), (1,)), ((), ())), preferred_element_type=jnp.float32)
            s = jnp.where(same, s * HD ** (-0.5), -1e30)
            e = jnp.exp(s - jnp.max(s, axis=1, keepdims=True))
            w = (e / jnp.sum(e, axis=1, keepdims=True)).astype(jnp.bfloat16)
            att[j * half : (j + 1) * half, part] = jnp.dot(
                w, v, preferred_element_type=jnp.float32
            ).astype(jnp.bfloat16)
    residual = res[...] + jnp.dot(att[...], outw_ref[...], preferred_element_type=jnp.float32)
    norm = lax.rsqrt(jnp.sum(residual * residual, axis=1, keepdims=True) / width + 1e-05)
    normed = (residual * norm * gain_ref[...]).astype(jnp.bfloat16)
    genes = jnp.dot(normed, dec_ref[...], preferred_element_type=jnp.float32).astype(jnp.bfloat16)
    for j in range(pair):
        out_ref[j] = genes[j * half : (j + 1) * half]


def shards(n, control, line_ids, pert_ids, pert_table, blocks, norm_gain, out_gain,
           qkv_weight, out_weight, decoder):
    lines, cells_here, width = control.shape
    cell_count = blocks.shape[1]
    sets = pert_ids.shape[0]
    inner_here = qkv_weight.shape[2]
    inner = 2 * inner_here
    genes = decoder.shape[1]
    hw = width // 2
    half = cell_count // 2
    m = lax.axis_index("mp")

    table_rows = pert_table.shape[0]
    offset = lax.axis_index("sets") * table_rows
    padded = -(-sets // 16) * 16
    ids = jnp.pad(pert_ids, (0, padded - sets), constant_values=-1)
    onehot = (
        ids[:, None] == offset + jnp.arange(table_rows, dtype=jnp.int32)[None, :]
    ).astype(jnp.bfloat16)
    table_half = lax.dynamic_slice_in_dim(pert_table, m * hw, hw, 1)
    rows = jnp.dot(onehot, table_half, preferred_element_type=jnp.float32).astype(jnp.bfloat16)
    extra = jnp.zeros((16, hw), jnp.bfloat16)
    extra = extra.at[0].set(line_ids[0].astype(jnp.bfloat16))
    extra = extra.at[1, :cell_count].set(blocks[0].astype(jnp.bfloat16))
    control_half = lax.dynamic_slice_in_dim(control, m * hw, hw, 2).reshape(lines * cells_here, hw)
    payload = jnp.concatenate([control_half, rows, extra], axis=0)
    height = payload.shape[0]

    any_spec = pl.BlockSpec(memory_space=pl.ANY)
    qkv_t = jnp.transpose(qkv_weight, (1, 0, 2))
    gathered, qkv_all, outw_all, dec_all = pl.pallas_call(
        functools.partial(gather_kernel, n),
        out_shape=(
            jax.ShapeDtypeStruct((2, n, height, hw), jnp.bfloat16),
            jax.ShapeDtypeStruct((2,) + qkv_t.shape, jnp.bfloat16),
            jax.ShapeDtypeStruct((2,) + out_weight.shape, jnp.bfloat16),
            jax.ShapeDtypeStruct((2,) + decoder.shape, jnp.bfloat16),
        ),
        in_specs=[any_spec] * 4,
        out_specs=(any_spec,) * 4,
        scratch_shapes=[
            pltpu.SemaphoreType.DMA((n, 4)),
            pltpu.SemaphoreType.DMA((2, n)),
            pltpu.SemaphoreType.DMA((3,)),
            pltpu.SemaphoreType.DMA((3,)),
            pltpu.SemaphoreType.DMA((4,)),
        ],
        compiler_params=pltpu.CompilerParams(
            collective_id=0, has_side_effects=True, vmem_limit_bytes=16 * MIB
        ),
    )(payload, qkv_t, out_weight, decoder)

    count = lines * cells_here
    cells = gathered[:, :, :count].reshape(2, n, lines, cells_here, hw)
    cells = jnp.transpose(cells, (2, 1, 3, 0, 4)).reshape(lines, cell_count, width)
    pert = jnp.sum(gathered[:, :, count : count + sets].astype(jnp.float32), axis=1)
    pert = jnp.transpose(pert, (1, 0, 2)).reshape(sets, width)
    line_all = gathered[0, :, count + padded, 0].astype(jnp.int32)
    blocks_all = gathered[0, :, count + padded + 1, :cell_count].astype(jnp.float32)
    own_blocks = lax.dynamic_slice_in_dim(blocks_all, m * half, half, 1)

    scaled = pert * norm_gain
    high = scaled.astype(jnp.bfloat16)
    low = (scaled - high.astype(jnp.float32)).astype(jnp.bfloat16)
    scaled_cells = (cells.astype(jnp.float32) * norm_gain).astype(jnp.bfloat16)
    lhs = jnp.concatenate([scaled_cells.reshape(-1, width), high, low], axis=0)
    projected = pl.pallas_call(
        project_kernel,
        grid=(6,),
        out_shape=jax.ShapeDtypeStruct((lhs.shape[0], 3 * inner), jnp.float32),
        in_specs=[
            pl.BlockSpec(lhs.shape, lambda i: (0, 0)),
            pl.BlockSpec((1, 1, width, inner_here), lambda i: (i % 2, i // 2, 0, 0)),
        ],
        out_specs=pl.BlockSpec((lhs.shape[0], inner_here), lambda i: (0, i)),
        compiler_params=pltpu.CompilerParams(vmem_limit_bytes=50 * MIB),
    )(lhs, qkv_all)
    base = lines * cell_count
    bias = projected[base : base + sets] + projected[base + sets : base + 2 * sets]

    pair = 2
    specs = []
    args = []
    for j in range(pair):
        specs += [
            pl.BlockSpec((1, cell_count, width), lambda i, r, j=j: (r[i * pair + j], 0, 0)),
            pl.BlockSpec((1, half, width), lambda i, r, j=j: (r[i * pair + j], r[sets], 0)),
            pl.BlockSpec((1, 1, width), lambda i, r, j=j: (i * pair + j, 0, 0)),
            pl.BlockSpec((half, inner), lambda i, r, j=j: (r[i * pair + j] * 2 + r[sets], 0)),
            pl.BlockSpec((cell_count, inner), lambda i, r, j=j: (r[i * pair + j], 1)),
            pl.BlockSpec((cell_count, inner), lambda i, r, j=j: (r[i * pair + j], 2)),
            pl.BlockSpec((1, 1, 3 * inner), lambda i, r, j=j: (i * pair + j, 0, 0)),
            pl.BlockSpec((1, 1, cell_count), lambda i, r, j=j: (i * pair + j, 0, 0)),
            pl.BlockSpec((1, half, 1), lambda i, r, j=j: (i * pair + j, 0, 0)),
        ]
        args += [
            cells, cells, pert[:, None, :], projected, projected, projected,
            bias[:, None, :], blocks_all[:, None, :], own_blocks[:, :, None],
        ]
    specs += [
        pl.BlockSpec((1, width), lambda i, r: (0, 0)),
        pl.BlockSpec((inner, width), lambda i, r: (0, 0), pipeline_mode=pl.Buffered(1)),
        pl.BlockSpec((width, genes), lambda i, r: (0, 0), pipeline_mode=pl.Buffered(1)),
    ]
    args += [out_gain[None], outw_all.reshape(inner, width), dec_all.reshape(width, genes)]
    return pl.pallas_call(
        functools.partial(layer_kernel, pair, width),
        grid_spec=pltpu.PrefetchScalarGridSpec(
            num_scalar_prefetch=1,
            grid=(sets // pair,),
            in_specs=specs,
            out_specs=pl.BlockSpec((pair, half, genes), lambda i, r: (i, 0, 0)),
            scratch_shapes=[
                pltpu.VMEM((pair * half, inner), jnp.bfloat16),
                pltpu.VMEM((pair * half, width), jnp.float32),
            ],
        ),
        out_shape=jax.ShapeDtypeStruct((sets, half, genes), jnp.bfloat16),
        compiler_params=pltpu.CompilerParams(vmem_limit_bytes=56 * MIB),
    )(jnp.concatenate([line_all, m[None].astype(jnp.int32)]), *args)


def solution(mesh):
    placed = (
        P("groups", "sets", None),
        P(("groups", "sets")),
        P("groups"),
        P("sets", None),
        P(("groups", "sets"), None),
        P(),
        P(),
        P(None, None, "mp"),
        P("mp", None),
        P("mp", "sets"),
    )
    return jax.shard_map(
        functools.partial(shards, mesh.shape["sets"]),
        mesh=mesh, in_specs=placed, out_specs=P("groups", "mp", "sets"), check_vma=False,
    )
```

time: 248 us -> 141 us (0.57)
  waiting for transfers between devices: 137 us -> 0 us
  Pallas kernels: 0 us -> 92.7 us
  blocking collectives: 42.1 us -> 0 us
  matrix products: 33.2 us -> 0.21 us
  local copies, waits for them, and re-layouts: 9.06 us -> 29.7 us
  between operations: 14 us -> 0.99 us
  other arithmetic: 11.5 us -> 16.4 us
    all_gather x2 -> x0, waiting for transfers between devices: 108 us -> none  [the longest x1 74.5 us: shards(): lax.all_gather(normed, 'sets', axis=0, tiled=True)]
    pallas_call x0 -> x3, Pallas kernels: none -> 92.7 us  [the longest x1 42.7 us: shards(): pl.pallas_call(functools.partial(gather_kernel, n), out_shape=(jax.ShapeD...]
    unnamed x1 -> x0, blocking collectives: 39.7 us -> none
    dot_general x7 -> x1, matrix products: 31.8 us -> 0.21 us  [shards(): jnp.dot(onehot, table_half, preferred_element_type=jnp.float32)]
    reduce_scatter x2 -> x0, waiting for transfers between devices: 27.9 us -> none  [the longest x1 19.9 us: shards(): lax.psum_scatter(gene_terms, 'mp', scatter_dimension=1, tiled=True)]
    unnamed x8 -> x17, local copies, waits for them, and re-layouts: 4.42 us -> 15.1 us
    reshape x1, local copies, waits for them, and re-layouts: 2.44 us -> 7.78 us  [shards(): jnp.transpose(cells, (2, 1, 3, 0, 4)).reshape(lines, cell_count, width)]
    convert_element_type x2 -> x6, other arithmetic: 7.34 us -> 12.4 us  [the longest x2 10.9 us: shards(): scaled_cells = (cells.astype(jnp.float32) * norm_gain).astype(jnp.bfloat16)]
  transfers between devices with their start and end apart: 4 -> 0, of which waited for: 4 -> 0; matrix products, arithmetic and copies ran while one was open for 2% -> 0% of each run, Pallas kernels for 0% -> 0%
where the time goes in v1:
time: 141 us; the launch traced here: 140 us
  Pallas kernels  92.7 us (66%)
  local copies, waits for them, and re-layouts  29.7 us (21%)
  other arithmetic  16.4 us (12%)
    pallas_call x1, Pallas kernels, shards(): pl.pallas_call(functools.partial(gather_kernel, n), out_shape=(jax.ShapeD...  42.7 us
    pallas_call x1, Pallas kernels, shards(): pl.pallas_call(functools.partial(layer_kernel, pair, width), grid_spec=pl...  31.3 us
    pallas_call x1, Pallas kernels, shards(): pl.pallas_call(project_kernel, grid=(6,), out_shape=jax.ShapeDtypeStruct(...  18.6 us
    unnamed x17, local copies, waits for them, and re-layouts  15.1 us
    convert_element_type x2, other arithmetic, shards(): scaled_cells = (cells.astype(jnp.float32) * norm_gain).astype(jnp.bfloat16)  10.9 us
    reshape x1, local copies, waits for them, and re-layouts, shards(): jnp.transpose(cells, (2, 1, 3, 0, 4)).reshape(lines, cell_count, width)  7.78 us

profile of v1, /device:TPU:0, one launch (start us, length us, event | category | flops | bytes accessed | tf_op | source)
XLA Modules:
  0.0 139.9 jit_solution(8648913440367923385)
XLA Ops:
  0.0 0.0 copy-start
  0.8 0.7 pad.10
  1.4 0.7 convert_element_type.59
  2.1 0.0 copy-done
  2.1 0.2 convolution_convert_fusion
  2.3 0.1 scatter.13
  2.4 0.2 scatter.14
  2.6 1.0 constant_dynamic-slice_fusion.1
  3.6 0.0 copy-start.3
  3.6 2.8 %copy-done.3 = bf16[2048,3,512]{2,0,1:T(8,128)(2,1)S(1)} copy-done((bf16[2048,3,512]{2,0,1:T(8,128)(2,1)S(1)}, bf16[2048,3,512]{2,0,1:T(8,128)(2,1)}, u32[]{:S(2)}) %copy-start.3) | copy-done | bytes 6291480
  6.4 1.9 %copy-done.5 = bf16[1024,1536]{1,0:T(8,128)(2,1)S(1)} copy-done((bf16[1024,1536]{1,0:T(8,128)(2,1)S(1)}, bf16[1024,1536]{1,0:T(8,128)(2,1)}, u32[]{:S(2)}) %copy-start.5) | copy-done | bytes 3145752
  8.3 1.6 %copy-done.6 = bf16[512,2048]{1,0:T(8,128)(2,1)S(1)} copy-done((bf16[512,2048]{1,0:T(8,128)(2,1)S(1)}, bf16[512,2048]{1,0:T(8,128)(2,1)}, u32[]{:S(2)}) %copy-start.6) | copy-done | bytes 2097176
  9.9 42.7 %shard_map.100 = (bf16[2,8,160,1024]{3,2,1,0:T(8,128)(2,1)S(1)}, bf16[2,3,2048,512]{3,2,1,0:T(8,128)(2,1)}, bf16[2,512,2048]{2,1,0:T(8,128)(2,1)S(1)}, bf16[2,1024,1536]{2,1,0:T(8,128)(2,1)S(1)}) custom-call(bf16[160,1024]{1,0:T(8,128)(2,1)S(1)} %pad_maximum_fusion.1.payload, bf16[3,2048,512]{2,1,0:T(8,128)(2,1)S(1)} %bitcast.21, ...), custom_call_target="tpu_custom_call" | custom-call | tf_op jit(solution)/shard_map/pallas_call | solution.py:225
  52.6 2.7 %copy-done.2 = bf16[2,1024,1536]{2,1,0:T(8,128)(2,1)} copy-done((bf16[2,1024,1536]{2,1,0:T(8,128)(2,1)}, bf16[2,1024,1536]{2,1,0:T(8,128)(2,1)S(1)}, u32[]{:S(2)}) %copy-start.2) | copy-done | bytes 6291480
  55.3 2.0 %copy-done.4 = bf16[2,512,2048]{2,1,0:T(8,128)(2,1)} copy-done((bf16[2,512,2048]{2,1,0:T(8,128)(2,1)}, bf16[2,512,2048]{2,1,0:T(8,128)(2,1)S(1)}, u32[]{:S(2)}) %copy-start.4) | copy-done | bytes 4194328
  57.3 0.2 convert_reduce_fusion.1
  57.5 0.7 pad_add_fusion.idx_ref
  58.2 0.6 slice_convert_fusion
  58.9 2.4 %slice.51 = bf16[2,8,128,1024]{3,2,1,0:T(8,128)(2,1)} slice(bf16[2,8,160,1024]{3,2,1,0:T(8,128)(2,1)S(1)} %get-tuple-element.33), slice={[0:2], [0:8], [0:128], [0:1024]} | slice | bytes 8388608 | tf_op jit(solution)/shard_map/slice | solution.py:248
  61.2 0.1 copy.16
  61.3 0.7 broadcast_in_dim_reshape.4.refs_2_.refs_11_
  62.1 1.0 copy.17.refs_8_.refs_17_
  63.1 9.7 %fusion.6 = (f32[4,8,32,2,1024]{4,3,2,1,0:T(2,128)S(1)}, bf16[4,8,32,2,1024]{4,3,2,1,0:T(2,128)(2,1)}) fusion(bf16[2,8,4,32,1024]{4,3,2,1,0:T(8,128)(2,1)} %bitcast.25), kind=kLoop, calls=%fused_computation.21 | loop fusion | flops 2097152 | bytes 16777216 | tf_op jit(solution)/shard_map/convert_element_type | solution.py:259
  72.7 4.1 %copy.19 = f32[128,8,2,1024]{3,1,2,0:T(8,128)S(1)} copy(f32[128,8,2,1024]{3,2,1,0:T(2,128)S(1)} %bitcast.23) | data formatting | bytes 16777216
  76.9 1.2 multiply_convert_fusion
  78.1 2.3 %pad_maximum_fusion.rows_ref = bf16[1040,2048]{1,0:T(8,128)(2,1)} fusion(bf16[8,2048]{1,0:T(8,128)(2,1)S(1)} %get-tuple-element.42, bf16[8,2048]{1,0:T(8,128)(2,1)S(1)} %get-tuple-element.41, bf16[1024,2048]{1,0:T(8,128)(2,1)S(1)} %multiply_convert_fusion), kind=kLoop, calls=%fused_computation.1 | loop fusion | flops 12779520 | bytes 8519680 | tf_op jit(solution)/shard_map/concatenate | solution.py:260
  80.4 18.6 %shard_map.101.refs_3_.refs_4_.refs_5_.refs_12_.refs_13_.refs_14_ = f32[1040,3072]{1,0:T(8,128)} custom-call(bf16[1040,2048]{1,0:T(8,128)(2,1)} %pad_maximum_fusion.rows_ref, bf16[2,3,2048,512]{3,2,1,0:T(8,128)(2,1)} %get-tuple-element.34.weight_ref), custom_call_target="tpu_custom_call" | custom-call | tf_op jit(solution)/shard_map/pallas_call | solution.py:261
  99.0 1.0 slice_add_fusion
  100.0 0.7 broadcast_in_dim.9.refs_6_.refs_15_
  100.7 7.8 %reshape.101.refs_0_.refs_1_.refs_9_.refs_10_ = bf16[4,256,2048]{2,1,0:T(8,128)(2,1)} reshape(bf16[4,8,32,2,1024]{4,3,2,1,0:T(2,128)(2,1)} %get-tuple-element.40) | data formatting | bytes 8388608 | tf_op jit(solution)/shard_map/reshape | solution.py:249
  108.4 31.3 %shard_map.102 = bf16[8,128,1536]{2,1,0:T(8,128)(2,1)} custom-call(s32[9]{0:T(128)} %pad_add_fusion.idx_ref, bf16[4,256,2048]{2,1,0:T(8,128)(2,1)} %reshape.101.refs_0_.refs_1_.refs_9_.refs_10_, bf16[4,256,2048]{2,1,0:T(8,128)(2,1)} %reshape.101.refs_0_.refs_1_.refs_9_.refs_10_, f32[8,1,2048]{2,1,0:T(1,128)} %broadcast_in_dim_reshape.4.refs_2_.refs_11_, ...), custom_call_target="tpu_custom_call" | custom-call | tf_op jit(solution)/shard_map/pallas_call | solution.py:300
  139.8 0.0 copy-done.1
  (13 shorter events, 0.1 us)
Async XLA Ops:
  0.0 2.1 %copy-start = (bf16[256,2048]{1,0:T(8,128)(2,1)S(1)}, bf16[256,2048]{1,0:T(8,128)(2,1)}, u32[]{:S(2)}) copy-start(bf16[256,2048]{1,0:T(8,128)(2,1)} %param.17) | copy-start | bytes 3145732
  3.6 2.8 %copy-start.3 = (bf16[2048,3,512]{2,0,1:T(8,128)(2,1)S(1)}, bf16[2048,3,512]{2,0,1:T(8,128)(2,1)}, u32[]{:S(2)}) copy-start(bf16[2048,3,512]{2,0,1:T(8,128)(2,1)} %param.21) | copy-start | bytes 18874372
  6.4 1.9 %copy-start.5 = (bf16[1024,1536]{1,0:T(8,128)(2,1)S(1)}, bf16[1024,1536]{1,0:T(8,128)(2,1)}, u32[]{:S(2)}) copy-start(bf16[1024,1536]{1,0:T(8,128)(2,1)} %dec.1) | copy-start | bytes 9437188
  8.3 1.6 %copy-start.6 = (bf16[512,2048]{1,0:T(8,128)(2,1)S(1)}, bf16[512,2048]{1,0:T(8,128)(2,1)}, u32[]{:S(2)}) copy-start(bf16[512,2048]{1,0:T(8,128)(2,1)} %outw.1) | copy-start | bytes 6291460
  52.6 2.7 %copy-start.2 = (bf16[2,1024,1536]{2,1,0:T(8,128)(2,1)}, bf16[2,1024,1536]{2,1,0:T(8,128)(2,1)S(1)}, u32[]{:S(2)}) copy-start(bf16[2,1024,1536]{2,1,0:T(8,128)(2,1)S(1)} %get-tuple-element.36) | copy-start | bytes 18874372
  55.3 2.0 %copy-start.4 = (bf16[2,512,2048]{2,1,0:T(8,128)(2,1)}, bf16[2,512,2048]{2,1,0:T(8,128)(2,1)S(1)}, u32[]{:S(2)}) copy-start(bf16[2,512,2048]{2,1,0:T(8,128)(2,1)S(1)} %get-tuple-element.35) | copy-start | bytes 12582916
  57.3 4.7 %copy-start.7 = (f32[2048]{0:T(1024)S(1)}, f32[2048]{0:T(1024)}, u32[]{:S(2)}) copy-start(f32[2048]{0:T(1024)} %param.19) | copy-start | bytes 24580
  108.4 31.3 %copy-start.1 = (bf16[256,2048]{1,0:T(8,128)(2,1)S(1)}, bf16[256,2048]{1,0:T(8,128)(2,1)}, u32[]{:S(2)}) copy-start(bf16[256,2048]{1,0:T(8,128)(2,1)} %param.17) | copy-start | bytes 3145732

commit v2 on v1

--- a/solution.py
+++ b/solution.py
@@ -152,44 +152,127 @@
         copy.wait()
 
 
-def project_kernel(rows_ref, weight_ref, out_ref):
-    out_ref[...] = jnp.dot(
-        rows_ref[...], weight_ref[0, 0], preferred_element_type=jnp.float32
-    )
-
-
-def layer_kernel(pair, width, idx_ref, *refs):
-    ins, (gain_ref, outw_ref, dec_ref, out_ref, att, res) = refs[: 9 * pair], refs[9 * pair :]
-    half = att.shape[0] // pair
-    inner = att.shape[1]
-    for j in range(pair):
-        c_ref, own_ref, p_ref, q_ref, k_ref, v_ref, b_ref, row_ref, col_ref = ins[9 * j : 9 * j + 9]
-        p = p_ref[0]
-        stream = c_ref[0].astype(jnp.float32) + p
-        scale = lax.rsqrt(jnp.sum(stream * stream, axis=1, keepdims=True) / width + 1e-05)
-        own = own_ref[0].astype(jnp.float32) + p
-        own_scale = lax.rsqrt(jnp.sum(own * own, axis=1, keepdims=True) / width + 1e-05)
-        res[j * half : (j + 1) * half, :] = own
-        same = col_ref[0] == row_ref[0]
-        b = b_ref[0]
-        for h in range(inner // HD):
-            part = slice(h * HD, (h + 1) * HD)
-            q = (own_scale * (q_ref[:, part] + b[:, part])).astype(jnp.bfloat16)
-            k = (scale * (k_ref[:, part] + b[:, inner + h * HD : inner + (h + 1) * HD])).astype(jnp.bfloat16)
-            v = (scale * (v_ref[:, part] + b[:, 2 * inner + h * HD : 2 * inner + (h + 1) * HD])).astype(jnp.bfloat16)
-            s = lax.dot_general(q, k, (((1,), (1,)), ((), ())), preferred_element_type=jnp.float32)
-            s = jnp.where(same, s * HD ** (-0.5), -1e30)
-            e = jnp.exp(s - jnp.max(s, axis=1, keepdims=True))
-            w = (e / jnp.sum(e, axis=1, keepdims=True)).astype(jnp.bfloat16)
-            att[j * half : (j + 1) * half, part] = jnp.dot(
-                w, v, preferred_element_type=jnp.float32
+def layer_kernel(n, lines, sets, pair, width, idx_ref, gath_ref, weight_ref, in_gain_ref,
+                 gain_ref, outw_hbm, dec_hbm, out_ref, cells, lhs, pert, proj_q, proj_kv, bias,
+                 labels, att, res, outw, dec, sem):
+    i = pl.program_id(0)
+    m = idx_ref[sets]
+    cell_count = cells.shape[1]
+    half = cell_count // 2
+    here = cell_count // n
+    hw = width // 2
+    inner_here = proj_q.shape[3]
+    count = lines * here
+    base = lines * cell_count
+    padded = -(-sets // 16) * 16
+    fetch = [
+        pltpu.make_async_copy(outw_hbm, outw, sem.at[0]),
+        pltpu.make_async_copy(dec_hbm, dec, sem.at[1]),
+    ]
+
+    @pl.when(i == 0)
+    def _():
+        for copy in fetch:
+            copy.start()
+        for h in range(2):
+            cols = slice(h * hw, (h + 1) * hw)
+            gain = in_gain_ref[:, cols]
+            total = jnp.zeros((sets, hw), jnp.float32)
+            for d in range(n):
+                for l in range(lines):
+                    block = gath_ref[h, d, l * here : (l + 1) * here, :]
+                    cells[l, d * here : (d + 1) * here, cols] = block
+                    at = l * cell_count + d * here
+                    lhs[at : at + here, cols] = (block.astype(jnp.float32) * gain).astype(jnp.bfloat16)
+                total += gath_ref[h, d, count : count + padded, :].astype(jnp.float32)[:sets]
+            for s in range(sets):
+                pert[s, :, cols] = total[s : s + 1]
+            scaled = total * gain
+            high = scaled.astype(jnp.bfloat16).astype(jnp.float32)
+            lhs[base : base + 2 * sets, cols] = jnp.concatenate(
+                [high, scaled - high], axis=0
             ).astype(jnp.bfloat16)
-    residual = res[...] + jnp.dot(att[...], outw_ref[...], preferred_element_type=jnp.float32)
-    norm = lax.rsqrt(jnp.sum(residual * residual, axis=1, keepdims=True) / width + 1e-05)
-    normed = (residual * norm * gain_ref[...]).astype(jnp.bfloat16)
-    genes = jnp.dot(normed, dec_ref[...], preferred_element_type=jnp.float32).astype(jnp.bfloat16)
-    for j in range(pair):
-        out_ref[j] = genes[j * half : (j + 1) * half]
+        for d in range(n):
+            slab = gath_ref[0, d, count + padded : count + padded + 16, :cell_count]
+            labels[d] = slab.astype(jnp.float32)[1:2]
+
+    def put_bias(terms):
+        total = terms[:sets] + terms[sets:]
+        for s in range(sets):
+            bias[i, s] = total[s : s + 1]
+
+    @pl.when(i < 2)
+    def _():
+        rows = [
+            lhs[pl.ds(pl.multiple_of(l * cell_count + m * half, half), half), :]
+            for l in range(lines)
+        ]
+        rows = jnp.concatenate(rows + [lhs[base:, :]], axis=0)
+        q = jnp.dot(rows, weight_ref[0, 0], preferred_element_type=jnp.float32)
+        for l in range(lines):
+            proj_q[i, l] = q[l * half : (l + 1) * half]
+        put_bias(q[lines * half :])
+
+    @pl.when((i >= 2) & (i < 6))
+    def _():
+        kv = jnp.dot(lhs[...], weight_ref[0, 0], preferred_element_type=jnp.float32)
+        for l in range(lines):
+            proj_kv[i - 2, l] = kv[l * cell_count : (l + 1) * cell_count]
+        put_bias(kv[base:])
+
+    @pl.when(i == 6)
+    def _():
+        for copy in fetch:
+            copy.wait()
+
+    @pl.when(i >= 6)
+    def _():
+        for j in range(pair):
+            s_at = (i - 6) * pair + j
+            line = idx_ref[s_at]
+            p = pert[s_at]
+            stream = cells[line].astype(jnp.float32) + p
+            scale = lax.rsqrt(jnp.sum(stream * stream, axis=1, keepdims=True) / width + 1e-05)
+            own = cells[line, pl.ds(pl.multiple_of(m * half, half), half), :].astype(jnp.float32) + p
+            own_scale = lax.rsqrt(jnp.sum(own * own, axis=1, keepdims=True) / width + 1e-05)
+            res[j * half : (j + 1) * half, :] = own
+            member = (
+                labels[s_at]
+                == lax.broadcasted_iota(jnp.int32, (8, cell_count), 0).astype(jnp.float32)
+            ).astype(jnp.float32)
+            mine = jnp.where(m == 0, member[:, :half], member[:, half:])
+            same = lax.dot_general(
+                mine, member, (((0,), (0,)), ((), ())), preferred_element_type=jnp.float32
+            ) > 0.5
+            for hh in range(2):
+                q_all = (own_scale * (proj_q[hh, line] + bias[hh, s_at])).astype(jnp.bfloat16)
+                k_all = (scale * (proj_kv[hh, line] + bias[2 + hh, s_at])).astype(jnp.bfloat16)
+                v_all = (scale * (proj_kv[2 + hh, line] + bias[4 + hh, s_at])).astype(jnp.bfloat16)
+                heads = inner_here // HD
+                parts = [slice(h * HD, (h + 1) * HD) for h in range(heads)]
+                scores = [
+                    lax.dot_general(
+                        q_all[:, part], k_all[:, part], (((1,), (1,)), ((), ())),
+                        preferred_element_type=jnp.float32,
+                    )
+                    for part in parts
+                ]
+                scores = [jnp.where(same, s * HD ** (-0.5), -1e30) for s in scores]
+                exps = [jnp.exp(s - jnp.max(s, axis=1, keepdims=True)) for s in scores]
+                weights = [
+                    (e * (1.0 / jnp.sum(e, axis=1, keepdims=True))).astype(jnp.bfloat16) for e in exps
+                ]
+                for h in range(heads):
+                    at = hh * inner_here + h * HD
+                    att[j * half : (j + 1) * half, at : at + HD] = jnp.dot(
+                        weights[h], v_all[:, parts[h]], preferred_element_type=jnp.float32
+                    ).astype(jnp.bfloat16)
+        residual = res[...] + jnp.dot(att[...], outw[...], preferred_element_type=jnp.float32)
+        norm = lax.rsqrt(jnp.sum(residual * residual, axis=1, keepdims=True) / width + 1e-05)
+        normed = (residual * norm * gain_ref[...]).astype(jnp.bfloat16)
+        genes = jnp.dot(normed, dec[...], preferred_element_type=jnp.float32).astype(jnp.bfloat16)
+        for j in range(pair):
+            out_ref[j] = genes[j * half : (j + 1) * half]
 
 
 def shards(n, control, line_ids, pert_ids, pert_table, blocks, norm_gain, out_gain,
@@ -240,78 +323,56 @@
             pltpu.SemaphoreType.DMA((4,)),
         ],
         compiler_params=pltpu.CompilerParams(
-            collective_id=0, has_side_effects=True, vmem_limit_bytes=16 * MIB
+            collective_id=0, has_side_effects=True, vmem_limit_bytes=60 * MIB
         ),
     )(payload, qkv_t, out_weight, decoder)
 
-    count = lines * cells_here
-    cells = gathered[:, :, :count].reshape(2, n, lines, cells_here, hw)
-    cells = jnp.transpose(cells, (2, 1, 3, 0, 4)).reshape(lines, cell_count, width)
-    pert = jnp.sum(gathered[:, :, count : count + sets].astype(jnp.float32), axis=1)
-    pert = jnp.transpose(pert, (1, 0, 2)).reshape(sets, width)
-    line_all = gathered[0, :, count + padded, 0].astype(jnp.int32)
-    blocks_all = gathered[0, :, count + padded + 1, :cell_count].astype(jnp.float32)
-    own_blocks = lax.dynamic_slice_in_dim(blocks_all, m * half, half, 1)
-
-    scaled = pert * norm_gain
-    high = scaled.astype(jnp.bfloat16)
-    low = (scaled - high.astype(jnp.float32)).astype(jnp.bfloat16)
-    scaled_cells = (cells.astype(jnp.float32) * norm_gain).astype(jnp.bfloat16)
-    lhs = jnp.concatenate([scaled_cells.reshape(-1, width), high, low], axis=0)
-    projected = pl.pallas_call(
-        project_kernel,
-        grid=(6,),
-        out_shape=jax.ShapeDtypeStruct((lhs.shape[0], 3 * inner), jnp.float32),
-        in_specs=[
-            pl.BlockSpec(lhs.shape, lambda i: (0, 0)),
-            pl.BlockSpec((1, 1, width, inner_here), lambda i: (i % 2, i // 2, 0, 0)),
-        ],
-        out_specs=pl.BlockSpec((lhs.shape[0], inner_here), lambda i: (0, i)),
-        compiler_params=pltpu.CompilerParams(vmem_limit_bytes=50 * MIB),
-    )(lhs, qkv_all)
-    base = lines * cell_count
-    bias = projected[base : base + sets] + projected[base + sets : base + 2 * sets]
-
+    line_all = gathered[0, :, lines * cells_here + padded, 0].astype(jnp.int32)
     pair = 2
-    specs = []
-    args = []
-    for j in range(pair):
-        specs += [
-            pl.BlockSpec((1, cell_count, width), lambda i, r, j=j: (r[i * pair + j], 0, 0)),
-            pl.BlockSpec((1, half, width), lambda i, r, j=j: (r[i * pair + j], r[sets], 0)),
-            pl.BlockSpec((1, 1, width), lambda i, r, j=j: (i * pair + j, 0, 0)),
-            pl.BlockSpec((half, inner), lambda i, r, j=j: (r[i * pair + j] * 2 + r[sets], 0)),
-            pl.BlockSpec((cell_count, inner), lambda i, r, j=j: (r[i * pair + j], 1)),
-            pl.BlockSpec((cell_count, inner), lambda i, r, j=j: (r[i * pair + j], 2)),
-            pl.BlockSpec((1, 1, 3 * inner), lambda i, r, j=j: (i * pair + j, 0, 0)),
-            pl.BlockSpec((1, 1, cell_count), lambda i, r, j=j: (i * pair + j, 0, 0)),
-            pl.BlockSpec((1, half, 1), lambda i, r, j=j: (i * pair + j, 0, 0)),
-        ]
-        args += [
-            cells, cells, pert[:, None, :], projected, projected, projected,
-            bias[:, None, :], blocks_all[:, None, :], own_blocks[:, :, None],
-        ]
-    specs += [
-        pl.BlockSpec((1, width), lambda i, r: (0, 0)),
-        pl.BlockSpec((inner, width), lambda i, r: (0, 0), pipeline_mode=pl.Buffered(1)),
-        pl.BlockSpec((width, genes), lambda i, r: (0, 0), pipeline_mode=pl.Buffered(1)),
-    ]
-    args += [out_gain[None], outw_all.reshape(inner, width), dec_all.reshape(width, genes)]
+    rows_all = lines * cell_count + 2 * sets
     return pl.pallas_call(
-        functools.partial(layer_kernel, pair, width),
+        functools.partial(layer_kernel, n, lines, sets, pair, width),
         grid_spec=pltpu.PrefetchScalarGridSpec(
             num_scalar_prefetch=1,
-            grid=(sets // pair,),
-            in_specs=specs,
-            out_specs=pl.BlockSpec((pair, half, genes), lambda i, r: (i, 0, 0)),
+            grid=(6 + sets // pair,),
+            in_specs=[
+                pl.BlockSpec(
+                    gathered.shape, lambda i, r: (0, 0, 0, 0), pipeline_mode=pl.Buffered(1)
+                ),
+                pl.BlockSpec(
+                    (1, 1, width, inner_here),
+                    lambda i, r: (jnp.minimum(i, 5) % 2, jnp.minimum(i, 5) // 2, 0, 0),
+                ),
+                pl.BlockSpec((1, width), lambda i, r: (0, 0)),
+                pl.BlockSpec((1, width), lambda i, r: (0, 0)),
+                any_spec,
+                any_spec,
+            ],
+            out_specs=pl.BlockSpec(
+                (pair, half, genes), lambda i, r: (jnp.maximum(i - 6, 0), 0, 0)
+            ),
             scratch_shapes=[
+                pltpu.VMEM((lines, cell_count, width), jnp.bfloat16),
+                pltpu.VMEM((rows_all, width), jnp.bfloat16),
+                pltpu.VMEM((sets, 1, width), jnp.float32),
+                pltpu.VMEM((2, lines, half, inner_here), jnp.float32),
+                pltpu.VMEM((4, lines, cell_count, inner_here), jnp.float32),
+                pltpu.VMEM((6, sets, 1, inner_here), jnp.float32),
+                pltpu.VMEM((sets, 1, cell_count), jnp.float32),
                 pltpu.VMEM((pair * half, inner), jnp.bfloat16),
                 pltpu.VMEM((pair * half, width), jnp.float32),
+                pltpu.VMEM((inner, width), jnp.bfloat16),
+                pltpu.VMEM((width, genes), jnp.bfloat16),
+                pltpu.SemaphoreType.DMA((2,)),
             ],
         ),
         out_shape=jax.ShapeDtypeStruct((sets, half, genes), jnp.bfloat16),
-        compiler_params=pltpu.CompilerParams(vmem_limit_bytes=56 * MIB),
-    )(jnp.concatenate([line_all, m[None].astype(jnp.int32)]), *args)
+        compiler_params=pltpu.CompilerParams(vmem_limit_bytes=60 * MIB),
+    )(
+        jnp.concatenate([line_all, m[None].astype(jnp.int32)]),
+        gathered, qkv_all, norm_gain[None], out_gain[None],
+        outw_all.reshape(inner, width), dec_all.reshape(width, genes),
+    )
 
 
 def solution(mesh):

time: 141 us -> 409 us (2.90)
  Pallas kernels: 92.7 us -> 403 us
  local copies, waits for them, and re-layouts: 29.7 us -> 1.91 us
  other arithmetic: 16.4 us -> 3.01 us
    pallas_call x1, Pallas kernels: 42.7 us -> 361 us  [shards(): pl.pallas_call(functools.partial(gather_kernel, n), out_shape=(jax.ShapeD...]
    unnamed x17 -> x2, local copies, waits for them, and re-layouts: 15.1 us -> 0.01 us
    convert_element_type x5 -> x1, other arithmetic: 11.8 us -> 0.95 us  [shards(): line_all = gathered[0, :, lines * cells_here + padded, 0].astype(jnp.int32)]
    pallas_call x2 -> x1, Pallas kernels: 50 us -> 42.1 us  [shards(): pl.pallas_call(functools.partial(layer_kernel, n, lines, sets, pair, widt...]
    reshape x1 -> x0, local copies, waits for them, and re-layouts: 7.78 us -> none  [shards(): jnp.transpose(cells, (2, 1, 3, 0, 4)).reshape(lines, cell_count, width)]
where the time goes in v2:
time: 409 us
  Pallas kernels  403 us (99%)
    pallas_call x1, Pallas kernels, shards(): pl.pallas_call(functools.partial(gather_kernel, n), out_shape=(jax.ShapeD...  361 us
    pallas_call x1, Pallas kernels, shards(): pl.pallas_call(functools.partial(layer_kernel, n, lines, sets, pair, widt...  42.1 us

profile of v2, /device:TPU:0, one launch (start us, length us, event | category | flops | bytes accessed | tf_op | source)
XLA Modules:
  0.0 409.0 jit_solution(13698392991250837613)
XLA Ops:
  0.0 0.0 copy-start
  0.8 0.7 pad.10
  1.4 0.7 convert_element_type.20
  2.1 0.0 copy-done
  2.1 0.2 convolution_convert_fusion
  2.3 0.1 scatter.13
  2.4 0.2 scatter.14
  2.6 1.0 constant_dynamic-slice_fusion
  3.6 0.7 pad_maximum_fusion.payload
  4.3 361.0 %shard_map.100 = (bf16[2,8,160,1024]{3,2,1,0:T(8,128)(2,1)}, bf16[2,3,2048,512]{3,2,1,0:T(8,128)(2,1)}, bf16[2,512,2048]{2,1,0:T(8,128)(2,1)}, bf16[2,1024,1536]{2,1,0:T(8,128)(2,1)}) custom-call(bf16[160,1024]{1,0:T(8,128)(2,1)} %pad_maximum_fusion.payload, bf16[3,2048,512]{2,1,0:T(8,128)(2,1)} %bitcast.7, bf16[512,2048]{1,0:T(8,128)(2,1)} %outw.1, ...), custom_call_target="tpu_custom_call" | custom-call | tf_op jit(solution)/shard_map/pallas_call | solution.py:308
  365.3 1.0 convert_reduce_fusion
  366.2 0.6 pad_add_fusion.idx_ref
  366.9 42.1 %shard_map.101 = bf16[8,128,1536]{2,1,0:T(8,128)(2,1)} custom-call(s32[9]{0:T(128)} %pad_add_fusion.idx_ref, bf16[2,8,160,1024]{3,2,1,0:T(8,128)(2,1)} %get-tuple-element.33.gath_ref, bf16[2,3,2048,512]{3,2,1,0:T(8,128)(2,1)} %get-tuple-element.34.weight_ref, f32[1,2048]{1,0:T(1,128)} %bitcast.11, f32[1,2048]{1,0:T(1,128)} %bitcast.12, ...), custom_call_target="tpu_custom_call" | custom-call | tf_op jit(solution)/shard_map/pallas_call | solution.py:333
  (2 shorter events, 0.0 us)
Async XLA Ops:
  0.0 2.1 copy-start

commit v3 on v2

--- a/solution.py
+++ b/solution.py
@@ -12,8 +12,8 @@
 MIB = 1024 * 1024
 
 
-def gather_kernel(n, payload, qkv, outw, dec, cells, qkv_all, outw_all, dec_all,
-                  send, recv, wsend, wrecv, local):
+def gather_kernel(n, payload, qkv, outw, dec, cells, qkv_peer, outw_peer, dec_peer,
+                  qkv_held, outw_held, dec_held, send, recv, wsend, wrecv, local):
     nz = n // 2
     me = lax.axis_index("sets")
     m = lax.axis_index("mp")
@@ -37,9 +37,9 @@
 
     own = [
         pltpu.make_async_copy(payload, cells.at[m, me], local.at[0]),
-        pltpu.make_async_copy(qkv, qkv_all.at[m], local.at[1]),
-        pltpu.make_async_copy(outw, outw_all.at[m], local.at[2]),
-        pltpu.make_async_copy(dec, dec_all.at[m], local.at[3]),
+        pltpu.make_async_copy(qkv, qkv_held, local.at[1]),
+        pltpu.make_async_copy(outw, outw_held, local.at[2]),
+        pltpu.make_async_copy(dec, dec_held, local.at[3]),
     ]
     for copy in own:
         copy.start()
@@ -109,13 +109,15 @@
     weights = [
         pltpu.make_async_remote_copy(
             src_ref=src,
-            dst_ref=dst.at[m],
+            dst_ref=dst,
             send_sem=wsend.at[i],
             recv_sem=wrecv.at[i],
             device_id=peer,
             device_id_type=MESH,
         )
-        for i, (src, dst) in enumerate(((qkv, qkv_all), (outw, outw_all), (dec, dec_all)))
+        for i, (src, dst) in enumerate(
+            ((qkv_held, qkv_peer), (outw_held, outw_peer), (dec_held, dec_peer))
+        )
     ]
 
     def start(copy):
@@ -131,7 +133,8 @@
         return cells.at[m, d]
 
     def after_own():
-        for copy in weights:
+        for held, copy in zip(own[1:], weights):
+            held.wait()
             copy.start()
 
     each(source, start)
@@ -148,12 +151,11 @@
         landed(1 - m, d)
     for copy in weights:
         copy.wait()
-    for copy in own:
-        copy.wait()
-
-
-def layer_kernel(n, lines, sets, pair, width, idx_ref, gath_ref, weight_ref, in_gain_ref,
-                 gain_ref, outw_hbm, dec_hbm, out_ref, cells, lhs, pert, proj_q, proj_kv, bias,
+    own[0].wait()
+
+
+def layer_kernel(n, lines, sets, pair, width, idx_ref, gath_ref, own_ref, peer_ref, in_gain_ref,
+                 gain_ref, outw_own, outw_peer, dec_own, dec_peer, out_ref, cells, lhs, pert, proj_q, proj_kv, bias,
                  labels, att, res, outw, dec, sem):
     i = pl.program_id(0)
     m = idx_ref[sets]
@@ -166,8 +168,12 @@
     base = lines * cell_count
     padded = -(-sets // 16) * 16
     fetch = [
-        pltpu.make_async_copy(outw_hbm, outw, sem.at[0]),
-        pltpu.make_async_copy(dec_hbm, dec, sem.at[1]),
+        pltpu.make_async_copy(outw_own, outw.at[:inner_here], sem.at[0]),
+        pltpu.make_async_copy(outw_peer, outw.at[inner_here:], sem.at[1]),
+        pltpu.make_async_copy(dec_own, dec.at[pl.ds(pl.multiple_of(m * hw, hw), hw)], sem.at[2]),
+        pltpu.make_async_copy(
+            dec_peer, dec.at[pl.ds(pl.multiple_of((1 - m) * hw, hw), hw)], sem.at[3]
+        ),
     ]
 
     @pl.when(i == 0)
@@ -201,24 +207,26 @@
         for s in range(sets):
             bias[i, s] = total[s : s + 1]
 
-    @pl.when(i < 2)
-    def _():
-        rows = [
-            lhs[pl.ds(pl.multiple_of(l * cell_count + m * half, half), half), :]
-            for l in range(lines)
-        ]
-        rows = jnp.concatenate(rows + [lhs[base:, :]], axis=0)
-        q = jnp.dot(rows, weight_ref[0, 0], preferred_element_type=jnp.float32)
-        for l in range(lines):
-            proj_q[i, l] = q[l * half : (l + 1) * half]
-        put_bias(q[lines * half :])
-
-    @pl.when((i >= 2) & (i < 6))
-    def _():
-        kv = jnp.dot(lhs[...], weight_ref[0, 0], preferred_element_type=jnp.float32)
-        for l in range(lines):
-            proj_kv[i - 2, l] = kv[l * cell_count : (l + 1) * cell_count]
-        put_bias(kv[base:])
+    for side, weight_ref in enumerate((own_ref, peer_ref)):
+
+        @pl.when(i == side)
+        def _(side=side, weight_ref=weight_ref):
+            rows = [
+                lhs[pl.ds(pl.multiple_of(l * cell_count + m * half, half), half), :]
+                for l in range(lines)
+            ]
+            rows = jnp.concatenate(rows + [lhs[base:, :]], axis=0)
+            q = jnp.dot(rows, weight_ref[0], preferred_element_type=jnp.float32)
+            for l in range(lines):
+                proj_q[side, l] = q[l * half : (l + 1) * half]
+            put_bias(q[lines * half :])
+
+        @pl.when((i >= 2) & (i < 6) & (i % 2 == side))
+        def _(weight_ref=weight_ref):
+            kv = jnp.dot(lhs[...], weight_ref[0], preferred_element_type=jnp.float32)
+            for l in range(lines):
+                proj_kv[i - 2, l] = kv[l * cell_count : (l + 1) * cell_count]
+            put_bias(kv[base:])
 
     @pl.when(i == 6)
     def _():
@@ -305,17 +313,20 @@
 
     any_spec = pl.BlockSpec(memory_space=pl.ANY)
     qkv_t = jnp.transpose(qkv_weight, (1, 0, 2))
-    gathered, qkv_all, outw_all, dec_all = pl.pallas_call(
+    gathered, qkv_peer, outw_peer, dec_peer = pl.pallas_call(
         functools.partial(gather_kernel, n),
         out_shape=(
             jax.ShapeDtypeStruct((2, n, height, hw), jnp.bfloat16),
-            jax.ShapeDtypeStruct((2,) + qkv_t.shape, jnp.bfloat16),
-            jax.ShapeDtypeStruct((2,) + out_weight.shape, jnp.bfloat16),
-            jax.ShapeDtypeStruct((2,) + decoder.shape, jnp.bfloat16),
+            jax.ShapeDtypeStruct(qkv_t.shape, jnp.bfloat16),
+            jax.ShapeDtypeStruct(out_weight.shape, jnp.bfloat16),
+            jax.ShapeDtypeStruct(decoder.shape, jnp.bfloat16),
         ),
-        in_specs=[any_spec] * 4,
-        out_specs=(any_spec,) * 4,
+        in_specs=[pl.BlockSpec(memory_space=pltpu.VMEM)] + [any_spec] * 3,
+        out_specs=(pl.BlockSpec(memory_space=pltpu.VMEM),) + (any_spec,) * 3,
         scratch_shapes=[
+            pltpu.VMEM(qkv_t.shape, jnp.bfloat16),
+            pltpu.VMEM(out_weight.shape, jnp.bfloat16),
+            pltpu.VMEM(decoder.shape, jnp.bfloat16),
             pltpu.SemaphoreType.DMA((n, 4)),
             pltpu.SemaphoreType.DMA((2, n)),
             pltpu.SemaphoreType.DMA((3,)),
@@ -339,12 +350,12 @@
                 pl.BlockSpec(
                     gathered.shape, lambda i, r: (0, 0, 0, 0), pipeline_mode=pl.Buffered(1)
                 ),
-                pl.BlockSpec(
-                    (1, 1, width, inner_here),
-                    lambda i, r: (jnp.minimum(i, 5) % 2, jnp.minimum(i, 5) // 2, 0, 0),
-                ),
+                pl.BlockSpec((1, width, inner_here), lambda i, r: (jnp.minimum(i // 2, 2), 0, 0)),
+                pl.BlockSpec((1, width, inner_here), lambda i, r: (jnp.minimum(i // 2, 2), 0, 0)),
                 pl.BlockSpec((1, width), lambda i, r: (0, 0)),
                 pl.BlockSpec((1, width), lambda i, r: (0, 0)),
+                any_spec,
+                any_spec,
                 any_spec,
                 any_spec,
             ],
@@ -363,15 +374,15 @@
                 pltpu.VMEM((pair * half, width), jnp.float32),
                 pltpu.VMEM((inner, width), jnp.bfloat16),
                 pltpu.VMEM((width, genes), jnp.bfloat16),
-                pltpu.SemaphoreType.DMA((2,)),
+                pltpu.SemaphoreType.DMA((4,)),
             ],
         ),
         out_shape=jax.ShapeDtypeStruct((sets, half, genes), jnp.bfloat16),
         compiler_params=pltpu.CompilerParams(vmem_limit_bytes=60 * MIB),
     )(
         jnp.concatenate([line_all, m[None].astype(jnp.int32)]),
-        gathered, qkv_all, norm_gain[None], out_gain[None],
-        outw_all.reshape(inner, width), dec_all.reshape(width, genes),
+        gathered, qkv_t, qkv_peer, norm_gain[None], out_gain[None],
+        out_weight, outw_peer, decoder, dec_peer,
     )
 
 

time: 409 us -> 96.9 us (0.24)
  Pallas kernels: 403 us -> 90.6 us
    pallas_call x1, Pallas kernels: 361 us -> 46.1 us  [shards(): pl.pallas_call(functools.partial(gather_kernel, n), out_shape=(jax.ShapeD...]
where the time goes in v3:
time: 96.9 us; the launch traced here: 96.6 us
  Pallas kernels  90.6 us (93%)
  other arithmetic  3.06 us (3%)
  local copies, waits for them, and re-layouts  1.91 us (2%)
    pallas_call x1, Pallas kernels, shards(): pl.pallas_call(functools.partial(gather_kernel, n), out_shape=(jax.ShapeD...  46.1 us
    pallas_call x1, Pallas kernels, shards(): pl.pallas_call(functools.partial(layer_kernel, n, lines, sets, pair, widt...  44.6 us

profile of v3, /device:TPU:0, one launch (start us, length us, event | category | flops | bytes accessed | tf_op | source)
XLA Modules:
  0.0 96.6 jit_solution(1103277798299032701)
XLA Ops:
  0.0 0.0 copy-start
  0.8 0.7 pad.10
  1.4 0.7 convert_element_type.20
  2.1 0.0 copy-done
  2.1 0.2 convolution_convert_fusion
  2.3 0.1 scatter.13
  2.4 0.2 scatter.14
  2.6 1.0 %constant_dynamic-slice_fusion = bf16[4,32,1024]{2,1,0:T(8,128)(2,1)S(1)} fusion(bf16[4,32,2048]{2,1,0:T(8,128)(2,1)} %param.14, s32[]{:T(128)S(6)} %select_n.4), kind=kLoop, calls=%fused_computation.10 | loop fusion | bytes 524292 | tf_op jit(solution)/shard_map/dynamic_slice | solution.py:310
  3.6 0.7 pad_maximum_fusion.payload
  4.3 46.1 %shard_map.100 = (bf16[2,8,160,1024]{3,2,1,0:T(8,128)(2,1)}, bf16[3,2048,512]{2,1,0:T(8,128)(2,1)}, bf16[512,2048]{1,0:T(8,128)(2,1)}, bf16[1024,1536]{1,0:T(8,128)(2,1)}) custom-call(bf16[160,1024]{1,0:T(8,128)(2,1)} %pad_maximum_fusion.payload, bf16[3,2048,512]{2,1,0:T(8,128)(2,1)} %bitcast.5, bf16[512,2048]{1,0:T(8,128)(2,1)} %outw_own.1, ...), custom_call_target="tpu_custom_call" | custom-call | tf_op jit(solution)/shard_map/pallas_call | solution.py:316
  50.4 1.0 convert_reduce_fusion
  51.4 0.7 pad_add_fusion.idx_ref
  52.0 44.6 %shard_map.101 = bf16[8,128,1536]{2,1,0:T(8,128)(2,1)} custom-call(s32[9]{0:T(128)} %pad_add_fusion.idx_ref, bf16[2,8,160,1024]{3,2,1,0:T(8,128)(2,1)} %get-tuple-element.33.gath_ref, bf16[3,2048,512]{2,1,0:T(8,128)(2,1)} %bitcast.6, bf16[3,2048,512]{2,1,0:T(8,128)(2,1)} %get-tuple-element.34.peer_ref, f32[1,2048]{1,0:T(1,128)} %bitcast.8, ...), custom_call_target="tpu_custom_call" | custom-call | tf_op jit(solution)/shard_map/pallas_call | solution.py:344
  (2 shorter events, 0.0 us)
Async XLA Ops:
  0.0 2.1 %copy-start = (bf16[256,2048]{1,0:T(8,128)(2,1)S(1)}, bf16[256,2048]{1,0:T(8,128)(2,1)}, u32[]{:S(2)}) copy-start(bf16[256,2048]{1,0:T(8,128)(2,1)} %param.17) | copy-start | bytes 3145732

commit v4 on v3

--- a/solution.py
+++ b/solution.py
@@ -8,6 +8,7 @@
 from jax.sharding import PartitionSpec as P
 
 HD = 128
+PIECES = 3
 MESH = pl.DeviceIdType.MESH
 MIB = 1024 * 1024
 
@@ -47,64 +48,72 @@
     neighbours = 2 + jnp.where(z < nz - 1, 1, 0) + jnp.where(z > 0, 1, 0)
     pl.semaphore_wait(barrier, neighbours)
 
-    def move(src, d, target, lane):
+    units = payload.shape[0] // 16
+    cuts = [16 * (units * q // PIECES) for q in range(PIECES + 1)]
+    spans = [pl.ds(cuts[q], cuts[q + 1] - cuts[q]) for q in range(PIECES)]
+
+    def move(src, d, target, lane, q):
         return pltpu.make_async_remote_copy(
-            src_ref=src,
-            dst_ref=cells.at[m, d],
-            send_sem=send.at[d, lane],
-            recv_sem=recv.at[m, d],
+            src_ref=src.at[spans[q]],
+            dst_ref=cells.at[m, d, spans[q]],
+            send_sem=send.at[d, lane, q],
+            recv_sem=recv.at[m, d, q],
             device_id=target,
             device_id_type=MESH,
         )
 
-    def landed(half, d):
+    def landed(half, d, q):
         pltpu.make_async_remote_copy(
-            src_ref=cells.at[half, d],
-            dst_ref=cells.at[half, d],
-            send_sem=send.at[d, 0],
-            recv_sem=recv.at[half, d],
+            src_ref=cells.at[half, d, spans[q]],
+            dst_ref=cells.at[half, d, spans[q]],
+            send_sem=send.at[d, 0, q],
+            recv_sem=recv.at[half, d, q],
             device_id=peer,
             device_id_type=MESH,
         ).wait_recv()
 
     def each(source, act):
         for k in range(nz):
+            for q in range(PIECES):
+                for sign in ((0,) if k == 0 else (-1, 1)):
+                    at = z + sign * k
+
+                    @pl.when((at >= 0) & (at < nz))
+                    def _(at=at, sign=sign, k=k, q=q):
+                        d = at * 2 + y
+                        src = source(d, k, q)
+                        if sign <= 0:
+
+                            @pl.when(z < nz - 1)
+                            def _():
+                                act(move(src, d, up, 0, q))
+
+                        if sign >= 0:
+
+                            @pl.when(z > 0)
+                            def _():
+                                act(move(src, d, down, 1, q))
+
+                        act(move(src, d, other, 2, q))
+                        act(move(src, d, peer, 3, q))
+
+            if k == 0:
+                after_own()
+            else:
+                crossing(k - 1, act)
+        crossing(nz - 1, act)
+
+    def crossing(k, act):
+        for q in range(PIECES):
             for sign in ((0,) if k == 0 else (-1, 1)):
                 at = z + sign * k
 
                 @pl.when((at >= 0) & (at < nz))
-                def _(at=at, sign=sign, k=k):
-                    d = at * 2 + y
-                    src = source(d, k)
-                    if sign <= 0:
-
-                        @pl.when(z < nz - 1)
-                        def _():
-                            act(move(src, d, up, 0))
-
-                    if sign >= 0:
-
-                        @pl.when(z > 0)
-                        def _():
-                            act(move(src, d, down, 1))
-
-                    act(move(src, d, other, 2))
-                    act(move(src, d, peer, 3))
-
-            if k == 0:
-                after_own()
-            crossing(k, act)
-
-    def crossing(k, act):
-        for sign in ((0,) if k == 0 else (-1, 1)):
-            at = z + sign * k
-
-            @pl.when((at >= 0) & (at < nz))
-            def _(at=at):
-                d = at * 2 + 1 - y
-                if act is start:
-                    landed(m, d)
-                act(move(cells.at[m, d], d, peer, 3))
+                def _(at=at, q=q):
+                    d = at * 2 + 1 - y
+                    if act is start:
+                        landed(m, d, q)
+                    act(move(cells.at[m, d], d, peer, 3, q))
 
     weights = [
         pltpu.make_async_remote_copy(
@@ -126,10 +135,10 @@
     def finish(copy):
         copy.wait_send()
 
-    def source(d, k):
+    def source(d, k, q):
         if k == 0:
             return payload
-        landed(m, d)
+        landed(m, d, q)
         return cells.at[m, d]
 
     def after_own():
@@ -139,7 +148,7 @@
 
     each(source, start)
 
-    def source(d, k):
+    def source(d, k, q):
         return payload if k == 0 else cells.at[m, d]
 
     def after_own():
@@ -148,7 +157,8 @@
     each(source, finish)
 
     for d in range(n):
-        landed(1 - m, d)
+        for q in range(PIECES):
+            landed(1 - m, d, q)
     for copy in weights:
         copy.wait()
     own[0].wait()
@@ -166,7 +176,7 @@
     inner_here = proj_q.shape[3]
     count = lines * here
     base = lines * cell_count
-    padded = -(-sets // 16) * 16
+    padded = -(-(sets + 2) // 16) * 16
     fetch = [
         pltpu.make_async_copy(outw_own, outw.at[:inner_here], sem.at[0]),
         pltpu.make_async_copy(outw_peer, outw.at[inner_here:], sem.at[1]),
@@ -199,8 +209,8 @@
                 [high, scaled - high], axis=0
             ).astype(jnp.bfloat16)
         for d in range(n):
-            slab = gath_ref[0, d, count + padded : count + padded + 16, :cell_count]
-            labels[d] = slab.astype(jnp.float32)[1:2]
+            slab = gath_ref[0, d, count : count + padded, :cell_count]
+            labels[d] = slab.astype(jnp.float32)[sets + 1 : sets + 2]
 
     def put_bias(terms):
         total = terms[:sets] + terms[sets:]
@@ -297,18 +307,17 @@
 
     table_rows = pert_table.shape[0]
     offset = lax.axis_index("sets") * table_rows
-    padded = -(-sets // 16) * 16
+    padded = -(-(sets + 2) // 16) * 16
     ids = jnp.pad(pert_ids, (0, padded - sets), constant_values=-1)
     onehot = (
         ids[:, None] == offset + jnp.arange(table_rows, dtype=jnp.int32)[None, :]
     ).astype(jnp.bfloat16)
     table_half = lax.dynamic_slice_in_dim(pert_table, m * hw, hw, 1)
     rows = jnp.dot(onehot, table_half, preferred_element_type=jnp.float32).astype(jnp.bfloat16)
-    extra = jnp.zeros((16, hw), jnp.bfloat16)
-    extra = extra.at[0].set(line_ids[0].astype(jnp.bfloat16))
-    extra = extra.at[1, :cell_count].set(blocks[0].astype(jnp.bfloat16))
+    rows = rows.at[sets].set(line_ids[0].astype(jnp.bfloat16))
+    rows = rows.at[sets + 1, :cell_count].set(blocks[0].astype(jnp.bfloat16))
     control_half = lax.dynamic_slice_in_dim(control, m * hw, hw, 2).reshape(lines * cells_here, hw)
-    payload = jnp.concatenate([control_half, rows, extra], axis=0)
+    payload = jnp.concatenate([control_half, rows], axis=0)
     height = payload.shape[0]
 
     any_spec = pl.BlockSpec(memory_space=pl.ANY)
@@ -327,8 +336,8 @@
             pltpu.VMEM(qkv_t.shape, jnp.bfloat16),
             pltpu.VMEM(out_weight.shape, jnp.bfloat16),
             pltpu.VMEM(decoder.shape, jnp.bfloat16),
-            pltpu.SemaphoreType.DMA((n, 4)),
-            pltpu.SemaphoreType.DMA((2, n)),
+            pltpu.SemaphoreType.DMA((n, 4, PIECES)),
+            pltpu.SemaphoreType.DMA((2, n, PIECES)),
             pltpu.SemaphoreType.DMA((3,)),
             pltpu.SemaphoreType.DMA((3,)),
             pltpu.SemaphoreType.DMA((4,)),
@@ -338,7 +347,7 @@
         ),
     )(payload, qkv_t, out_weight, decoder)
 
-    line_all = gathered[0, :, lines * cells_here + padded, 0].astype(jnp.int32)
+    line_all = gathered[0, :, lines * cells_here + sets, 0].astype(jnp.int32)
     pair = 2
     rows_all = lines * cell_count + 2 * sets
     return pl.pallas_call(

time: 96.9 us -> 86.4 us (0.89)
  Pallas kernels: 90.6 us -> 80.2 us
    pallas_call x1, Pallas kernels: 46.1 us -> 35.8 us  [shards(): pl.pallas_call(functools.partial(gather_kernel, n), out_shape=(jax.ShapeD...]
where the time goes in v4:
time: 86.4 us; the launch traced here: 86.1 us
  Pallas kernels  80.2 us (93%)
  other arithmetic  2.96 us (3%)
  local copies, waits for them, and re-layouts  1.94 us (2%)
    pallas_call x1, Pallas kernels, shards(): pl.pallas_call(functools.partial(layer_kernel, n, lines, sets, pair, widt...  44.4 us
    pallas_call x1, Pallas kernels, shards(): pl.pallas_call(functools.partial(gather_kernel, n), out_shape=(jax.ShapeD...  35.8 us

profile of v4, /device:TPU:0, one launch (start us, length us, event | category | flops | bytes accessed | tf_op | source)
XLA Modules:
  0.0 86.1 jit_solution(5622121500621514498)
XLA Ops:
  0.0 0.0 copy-start
  0.7 0.7 pad.9
  1.4 0.7 convert_element_type.23
  2.1 0.0 copy-done
  2.1 0.2 convolution_convert_fusion
  2.3 0.1 scatter.6
  2.4 0.2 scatter.9
  2.6 1.0 %constant_dynamic-slice_fusion = bf16[4,32,1024]{2,1,0:T(8,128)(2,1)S(1)} fusion(bf16[4,32,2048]{2,1,0:T(8,128)(2,1)} %param.14, s32[]{:T(128)S(6)} %select_n.4), kind=kLoop, calls=%fused_computation.10 | loop fusion | bytes 524292 | tf_op jit(solution)/shard_map/dynamic_slice | solution.py:319
  3.6 0.7 pad_maximum_fusion.payload
  4.3 35.8 %shard_map.100 = (bf16[2,8,144,1024]{3,2,1,0:T(8,128)(2,1)}, bf16[3,2048,512]{2,1,0:T(8,128)(2,1)}, bf16[512,2048]{1,0:T(8,128)(2,1)}, bf16[1024,1536]{1,0:T(8,128)(2,1)}) custom-call(bf16[144,1024]{1,0:T(8,128)(2,1)} %pad_maximum_fusion.payload, bf16[3,2048,512]{2,1,0:T(8,128)(2,1)} %bitcast.6, bf16[512,2048]{1,0:T(8,128)(2,1)} %outw_own.1, ...), custom_call_target="tpu_custom_call" | custom-call | tf_op jit(solution)/shard_map/pallas_call | solution.py:325
  40.1 1.0 %convert_reduce_fusion = s32[8]{0:T(128)S(1)} fusion(bf16[2,8,144,1024]{3,2,1,0:T(8,128)(2,1)} %get-tuple-element.33.gath_ref), kind=kLoop, calls=%fused_computation.6 | loop fusion | flops 8 | bytes 48 | tf_op jit(solution)/shard_map/convert_element_type | solution.py:350
  41.1 0.6 pad_add_fusion.idx_ref
  41.7 44.4 %shard_map.101 = bf16[8,128,1536]{2,1,0:T(8,128)(2,1)} custom-call(s32[9]{0:T(128)} %pad_add_fusion.idx_ref, bf16[2,8,144,1024]{3,2,1,0:T(8,128)(2,1)} %get-tuple-element.33.gath_ref, bf16[3,2048,512]{2,1,0:T(8,128)(2,1)} %bitcast.7, bf16[3,2048,512]{2,1,0:T(8,128)(2,1)} %get-tuple-element.34.peer_ref, f32[1,2048]{1,0:T(1,128)} %bitcast.9, ...), custom_call_target="tpu_custom_call" | custom-call | tf_op jit(solution)/shard_map/pallas_call | solution.py:353
  (2 shorter events, 0.0 us)
Async XLA Ops:
  0.0 2.1 %copy-start = (bf16[256,2048]{1,0:T(8,128)(2,1)S(1)}, bf16[256,2048]{1,0:T(8,128)(2,1)}, u32[]{:S(2)}) copy-start(bf16[256,2048]{1,0:T(8,128)(2,1)} %param.17) | copy-start | bytes 3145732

commit v5 on v4

--- a/solution.py
+++ b/solution.py
@@ -348,7 +348,7 @@
     )(payload, qkv_t, out_weight, decoder)
 
     line_all = gathered[0, :, lines * cells_here + sets, 0].astype(jnp.int32)
-    pair = 2
+    pair = 4 if sets % 4 == 0 else 2
     rows_all = lines * cell_count + 2 * sets
     return pl.pallas_call(
         functools.partial(layer_kernel, n, lines, sets, pair, width),

time: 86.4 us -> 85.3 us (0.987)
  Pallas kernels: 80.2 us -> 79.1 us
    pallas_call x1, Pallas kernels: 44.4 us -> 43.4 us  [shards(): pl.pallas_call(functools.partial(layer_kernel, n, lines, sets, pair, widt...]
where the time goes in v5:
time: 85.3 us; the launch traced here: 85 us
  Pallas kernels  79.1 us (93%)
  other arithmetic  2.96 us (3%)
  local copies, waits for them, and re-layouts  1.94 us (2%)
    pallas_call x1, Pallas kernels, shards(): pl.pallas_call(functools.partial(layer_kernel, n, lines, sets, pair, widt...  43.4 us
    pallas_call x1, Pallas kernels, shards(): pl.pallas_call(functools.partial(gather_kernel, n), out_shape=(jax.ShapeD...  35.8 us

profile of v5, /device:TPU:0, one launch (start us, length us, event | category | flops | bytes accessed | tf_op | source)
XLA Modules:
  0.0 85.0 jit_solution(17600350044330969583)
XLA Ops:
  0.0 0.0 copy-start
  0.7 0.7 pad.9
  1.4 0.7 convert_element_type.23
  2.1 0.0 copy-done
  2.1 0.2 convolution_convert_fusion
  2.3 0.1 scatter.6
  2.4 0.2 scatter.9
  2.6 1.0 %constant_dynamic-slice_fusion = bf16[4,32,1024]{2,1,0:T(8,128)(2,1)S(1)} fusion(bf16[4,32,2048]{2,1,0:T(8,128)(2,1)} %param.14, s32[]{:T(128)S(6)} %select_n.4), kind=kLoop, calls=%fused_computation.10 | loop fusion | bytes 524292 | tf_op jit(solution)/shard_map/dynamic_slice | solution.py:319
  3.6 0.7 pad_maximum_fusion.payload
  4.3 35.8 %shard_map.100 = (bf16[2,8,144,1024]{3,2,1,0:T(8,128)(2,1)}, bf16[3,2048,512]{2,1,0:T(8,128)(2,1)}, bf16[512,2048]{1,0:T(8,128)(2,1)}, bf16[1024,1536]{1,0:T(8,128)(2,1)}) custom-call(bf16[144,1024]{1,0:T(8,128)(2,1)} %pad_maximum_fusion.payload, bf16[3,2048,512]{2,1,0:T(8,128)(2,1)} %bitcast.6, bf16[512,2048]{1,0:T(8,128)(2,1)} %outw_own.1, ...), custom_call_target="tpu_custom_call" | custom-call | tf_op jit(solution)/shard_map/pallas_call | solution.py:325
  40.1 1.0 %convert_reduce_fusion = s32[8]{0:T(128)S(1)} fusion(bf16[2,8,144,1024]{3,2,1,0:T(8,128)(2,1)} %get-tuple-element.33.gath_ref), kind=kLoop, calls=%fused_computation.6 | loop fusion | flops 8 | bytes 48 | tf_op jit(solution)/shard_map/convert_element_type | solution.py:350
  41.1 0.6 pad_add_fusion.idx_ref
  41.7 43.4 %shard_map.101 = bf16[8,128,1536]{2,1,0:T(8,128)(2,1)} custom-call(s32[9]{0:T(128)} %pad_add_fusion.idx_ref, bf16[2,8,144,1024]{3,2,1,0:T(8,128)(2,1)} %get-tuple-element.33.gath_ref, bf16[3,2048,512]{2,1,0:T(8,128)(2,1)} %bitcast.7, bf16[3,2048,512]{2,1,0:T(8,128)(2,1)} %get-tuple-element.34.peer_ref, f32[1,2048]{1,0:T(1,128)} %bitcast.9, ...), custom_call_target="tpu_custom_call" | custom-call | tf_op jit(solution)/shard_map/pallas_call | solution.py:353
  (2 shorter events, 0.0 us)
Async XLA Ops:
  0.0 2.1 %copy-start = (bf16[256,2048]{1,0:T(8,128)(2,1)S(1)}, bf16[256,2048]{1,0:T(8,128)(2,1)}, u32[]{:S(2)}) copy-start(bf16[256,2048]{1,0:T(8,128)(2,1)} %param.17) | copy-start | bytes 3145732
